TPU v7x, 32 devices: a whole 2x2x4 slice. The times are simulated.
32 devices in a mesh: seq: 8 (over y, x, core), head: 4 (over z).
Axes of the slice: x: 2, y: 2, z: 4, core: 2. Of those that a mesh axis runs over, the one named last changes fastest.
Arguments:
- mixer_input: bfloat16 [12288, 4096], P('seq', 'head'), may hold values from -6 to 6
- gate_input: bfloat16 [12288, 4096], P('seq', 'head'), may hold values from -6 to 6
- state_maps: bfloat16 [4, 12288, 128], P(None, 'seq'), may hold values from -0.375 to 0.375
- step_size: float32 [2, 64, 12288], P(None, 'head', 'seq'), may hold values from 0.2 to 2
- log_decay: float32 [2, 64, 12288], P(None, 'head', 'seq'), may hold values from -2 to 0
- skip_weight: float32 [64], P('head'), may hold values from 0.5 to 1.5
- doc_ids: int32 [12288], P('seq'), may hold values from 0 to 3, never falling along the last dimension, each value on 1 to 6144 neighbouring positions
- norm_gain: float32 [4096], P('head'), may hold values from 0.1 to 1.9
Outputs:
- mixed: bfloat16 [12288, 4096], P('seq', 'head')
Inputs may be any that keep to these rules, and one draw needn't show every extreme that they name: `doc_ids`: ids never fall along the sequence; each of the 4 documents holds 1 to 6144 tokens, one exactly 6144.
All inputs are finite; a program needn't handle non-finite values.
Results may differ from a plain program's by a relative error of at most 0.0054.
Values sent between devices are 32-bit elements; how exact they have to be, the bound alone decides.
A program may use at most 256 MiB of HBM per device.

v0:
```python
import jax
import jax.numpy as jnp
from jax import lax
from jax.sharding import PartitionSpec as P

BLOCK = 128


def prefix(part, axis, combine, identity, reverse):
    count = lax.axis_size(axis)
    place = lax.axis_index(axis)
    ahead = count - 1 - place if reverse else place
    gathered = jax.tree.map(lambda a: lax.all_gather(a, axis), part)
    state = jax.tree.map(lambda a, e: jnp.zeros_like(a) + jnp.asarray(e, a.dtype), part, identity)

    def one(step, state):
        source = count - 1 - step if reverse else step
        return combine(
            state, jax.tree.map(lambda a: lax.dynamic_index_in_dim(a, source, 0, False), gathered)
        )

    return lax.fori_loop(0, ahead, one, state)


def combine(earlier, later):
    decay_first, state_first, enter_first, leave_first = earlier
    decay_second, state_second, enter_second, leave_second = later
    keeping = ((leave_first == enter_second) | (enter_first < 0.0) | (enter_second < 0.0)).astype(
        jnp.float32
    )
    carried = decay_second * keeping
    return (
        carried * decay_first,
        state_second + carried[:, None, None] * state_first,
        jnp.where(enter_first < 0.0, enter_second, enter_first),
        jnp.where(leave_second < 0.0, leave_first, leave_second),
    )


def local_pass(blocks_x, b_rows, c_rows, decay_rows, step_rows, doc_rows):
    block_count = blocks_x.shape[0]
    head_count = decay_rows.shape[0]
    b_blocks = b_rows.reshape(block_count, BLOCK, -1)
    c_blocks = c_rows.reshape(block_count, BLOCK, -1)
    cumulative = jnp.cumsum(decay_rows.reshape(head_count, block_count, BLOCK), axis=2)
    step_blocks = step_rows.reshape(head_count, block_count, BLOCK)
    doc_blocks = doc_rows.reshape(block_count, BLOCK)
    scores = jnp.einsum("btn,bsn->bts", c_blocks, b_blocks, preferred_element_type=jnp.float32)
    places = jnp.arange(BLOCK)
    strict = (places[:, None] > places[None, :])[None] & (
        doc_blocks[:, :, None] == doc_blocks[:, None, :]
    )
    spread = jnp.where(strict[None], cumulative[:, :, :, None] - cumulative[:, :, None, :], 0.0)
    weights = jnp.where(
        strict[None], scores[None] * jnp.exp(spread) * step_blocks[:, :, None, :], 0.0
    )
    weights = weights.astype(jnp.bfloat16)
    inside_out = jnp.einsum(
        "hbts,bshp->bthp", weights, blocks_x, preferred_element_type=jnp.float32
    )
    last_ids = doc_blocks[:, -1]
    same_end = doc_blocks == last_ids[:, None]
    to_end = jnp.where(
        same_end[None], jnp.exp(cumulative[:, :, -1:] - cumulative) * step_blocks, 0.0
    )
    weighted_b = (b_blocks.astype(jnp.float32)[None] * to_end[..., None]).astype(jnp.bfloat16)
    local_states = jnp.einsum(
        "hbsn,bshp->bhnp", weighted_b, blocks_x, preferred_element_type=jnp.float32
    )
    prior_ids = jnp.concatenate([doc_rows[:1], last_ids[:-1]])
    block_decay = (
        jnp.exp(cumulative[:, :, -1]).T * (last_ids == prior_ids).astype(jnp.float32)[:, None]
    )

    def advance(carried_pair, block_item):
        state_now, factor_now = carried_pair
        local_now, decay_now = block_item
        return (
            (decay_now[:, None, None] * state_now + local_now, factor_now * decay_now),
            (state_now, factor_now),
        )

    start_state = jnp.zeros(local_states.shape[1:], jnp.float32)
    start_factor = jnp.ones((head_count,), jnp.float32)
    (final_state, total_decay), (starts, factors) = lax.scan(
        advance, (start_state, start_factor), (local_states, block_decay)
    )
    summary = (
        total_decay,
        final_state,
        doc_rows[:1].astype(jnp.float32),
        doc_rows[-1:].astype(jnp.float32),
    )
    return (inside_out, cumulative, starts, factors, prior_ids, summary)


def finish(c_rows, doc_rows, parts, incoming):
    inside_out, cumulative, starts, factors, prior_ids, summary = parts
    block_count = starts.shape[0]
    matching = (incoming[3] == doc_rows[:1].astype(jnp.float32)).astype(jnp.float32)
    arriving = incoming[1] * matching[:, None, None]
    entering = (starts + factors[:, :, None, None] * arriving[None]).astype(jnp.bfloat16)
    c_blocks = c_rows.reshape(block_count, BLOCK, -1)
    carried = jnp.einsum("btn,bhnp->bthp", c_blocks, entering, preferred_element_type=jnp.float32)
    doc_blocks = doc_rows.reshape(block_count, BLOCK)
    same_doc = (doc_blocks == prior_ids[:, None]).astype(jnp.float32)
    carry_reach = jnp.exp(cumulative).transpose(1, 2, 0) * same_doc[:, :, None]
    return inside_out + carried * carry_reach[..., None]


def local(
    mixer_input, gate_input, state_maps, step_size, log_decay, skip_weight, doc_ids, norm_gain
):
    tokens = mixer_input.shape[0]
    head_count = step_size.shape[1]
    head_width = mixer_input.shape[1] // head_count
    state_dim = state_maps.shape[2]
    block_count = tokens // BLOCK
    per_token = mixer_input.reshape(tokens, head_count, head_width)
    forward_x = per_token.reshape(block_count, BLOCK, head_count, head_width)
    backward_x = per_token[::-1].reshape(block_count, BLOCK, head_count, head_width)
    reversed_docs = doc_ids[::-1]
    reversed_c = state_maps[3][::-1]
    fwd_parts = local_pass(
        forward_x, state_maps[0], state_maps[1], log_decay[0], step_size[0], doc_ids
    )
    bwd_parts = local_pass(
        backward_x,
        state_maps[2][::-1],
        reversed_c,
        log_decay[1][:, ::-1],
        step_size[1][:, ::-1],
        reversed_docs,
    )
    fwd_sum = fwd_parts[5]
    bwd_sum = bwd_parts[5]
    neutral = (
        jnp.ones((head_count,), jnp.float32),
        jnp.zeros((head_count, state_dim, head_width), jnp.float32),
        -jnp.ones((1,), jnp.float32),
        -jnp.ones((1,), jnp.float32),
    )
    fwd_in = prefix(
        (fwd_sum[0], fwd_sum[1], fwd_sum[2], fwd_sum[3]), "seq", combine, neutral, False
    )
    bwd_in = prefix((bwd_sum[0], bwd_sum[1], bwd_sum[2], bwd_sum[3]), "seq", combine, neutral, True)
    forward_out = finish(state_maps[1], doc_ids, fwd_parts, fwd_in).reshape(
        tokens, head_count, head_width
    )
    backward_out = finish(reversed_c, reversed_docs, bwd_parts, bwd_in).reshape(
        tokens, head_count, head_width
    )[::-1]
    combined = (
        forward_out + backward_out + skip_weight[None, :, None] * per_token.astype(jnp.float32)
    )
    gate_wide = gate_input.astype(jnp.float32).reshape(tokens, head_count, head_width)
    gated_out = (combined * jax.nn.silu(gate_wide)).reshape(tokens, head_count * head_width)
    partial_squares = jnp.sum(gated_out * gated_out, axis=1)
    square_total = lax.psum(partial_squares, "head")
    channels = lax.axis_size("head") * head_count * head_width
    inverse_rms = lax.rsqrt(square_total / channels + 1e-05)
    return (gated_out * inverse_rms[:, None] * norm_gain[None, :]).astype(jnp.bfloat16)


def solution(mesh):
    return jax.shard_map(
        local,
        mesh=mesh,
        in_specs=(
            P("seq", "head"),
            P("seq", "head"),
            P(None, "seq", None),
            P(None, "head", "seq"),
            P(None, "head", "seq"),
            P("head"),
            P("seq"),
            P("head"),
        ),
        out_specs=P("seq", "head"),
        check_vma=False,
    )
```

profile of v0, /device:TPU:0, one launch (start us, length us, event | category | flops | bytes accessed | tf_op | source)
XLA Modules:
  0.0 315.6 jit_solution(17336573197923804926)
XLA Ops:
  15.4 4.6 %copy.124 = bf16[1536,1024]{0,1:T(8,128)(2,1)} copy(bf16[1536,1024]{1,0:T(8,128)(2,1)} %param.16) | data formatting | bytes 6291456 | tf_op args[0]
  20.0 4.5 %reduce_window_sum.17 = f32[16,12,128]{2,1,0:T(8,128)S(1)} reduce-window(f32[16,12,128]{2,1,0:T(8,128)S(1)} %reshape_squeeze.13, f32[]{:T(128)} %constant.111.clone.1), window={size=1x1x128 pad=0_0x0_0x127_0}, to_apply=%region_0.0 | reduce-window | flops 3121152 | bytes 196612 | tf_op jit(solution)/shard_map/jit(cumsum)/reduce_window_sum | solution.py:45
  26.4 6.9 %reshape_reshape.3 = bf16[12,128,16,64]{1,0,3,2:T(8,128)(2,1)} reshape(bf16[1536,1024]{0,1:T(8,128)(2,1)} %copy.124) | data formatting | bytes 6291456 | tf_op jit(solution)/shard_map/reshape;reshape | solution.py:120
  34.1 10.4 %fusion.16 = f32[12,16,128,64]{3,2,1,0:T(8,128)} fusion(f32[16,12,128]{2,0,1:T(8,128)S(1)} %copy.126, f32[12,128,128]{2,1,0:T(8,128)S(1)} %convert_element_type.77, bf16[12,128,16,64]{1,0,3,2:T(8,128)(2,1)} %reshape_reshape.3), kind=kOutput, calls=%fused_computation.42 | convolution fusion | flops 408944640 | bytes 10321920 | tf_op jit(solution)/shard_map/hbsn,bshp->bhnp/dot_general | solution.py:67
  44.5 6.1 %broadcast.140.clone.1 = f32[12,16,128,64]{3,2,1,0:T(8,128)} broadcast(f32[]{:T(128)} %constant.111.clone.1), dimensions={} | broadcast | bytes 6291460 | tf_op jit(solution)/shard_map/broadcast.7
  50.6 30.8 %while.70 = (s32[]{:T(128)}, f32[16,128,64]{2,1,0:T(8,128)S(1)}, f32[16]{0:T(128)S(1)}, f32[12,16,128,64]{3,2,1,0:T(8,128)}, f32[12,16]{1,0:T(8,128)S(1)}, /*ind...) while((s32[]{:T(128)}, f32[16,128,64]{2,1,0:T(8,128)S(1)}, ...), condition=%wide.region_2.3_spmd.clone, body=%wide.region_1.2_spmd.clone.sunk | while | flops 524323 | bytes 3146869 | solution.py:85
  83.8 4.6 %reduce_window_sum.18 = f32[16,12,128]{2,1,0:T(8,128)S(1)} reduce-window(f32[16,12,128]{2,1,0:T(8,128)S(1)} %reshape.215, f32[]{:T(128)} %constant.111.clone.1), window={size=1x1x128 pad=0_0x0_0x127_0}, to_apply=%region_5.6 | reduce-window | flops 3121152 | bytes 196612 | tf_op jit(solution)/shard_map/jit(cumsum)/reduce_window_sum | solution.py:45
  92.1 8.8 %rev.26 = bf16[1536,16,64]{0,2,1:T(8,128)(2,1)} reverse(bf16[1536,16,64]{0,2,1:T(8,128)(2,1)} %bitcast.170), dimensions={0} | reverse | bytes 6291456 | tf_op jit(solution)/shard_map/rev | solution.py:121
  102.4 10.3 %fusion.18 = f32[12,16,128,64]{3,2,1,0:T(8,128)} fusion(f32[16,12,128]{2,0,1:T(8,128)} %copy.140, f32[12,128,128]{2,1,0:T(8,128)S(1)} %convert_element_type.84, bf16[1536,16,64]{0,2,1:T(8,128)(2,1)} %rev.26), kind=kOutput, calls=%fused_computation.44 | convolution fusion | flops 408944640 | bytes 10321920 | tf_op jit(solution)/shard_map/hbsn,bshp->bhnp/dot_general | solution.py:67
  112.7 6.1 %broadcast.140.clone = f32[12,16,128,64]{3,2,1,0:T(8,128)} broadcast(f32[]{:T(128)} %constant.111.clone.1), dimensions={} | broadcast | bytes 6291460 | tf_op jit(solution)/shard_map/broadcast.7
  118.8 30.9 %while.71 = (s32[]{:T(128)}, f32[16,128,64]{2,1,0:T(8,128)S(1)}, f32[16]{0:T(128)S(1)}, f32[12,16,128,64]{3,2,1,0:T(8,128)}, f32[12,16]{1,0:T(8,128)S(1)}, /*ind...) while((s32[]{:T(128)}, f32[16,128,64]{2,1,0:T(8,128)S(1)}, ...), condition=%wide.region_7.8_spmd.clone, body=%wide.region_6.7_spmd.clone.sunk | while | flops 524323 | bytes 3146869 | solution.py:85
  155.5 15.5 %all-reduce.4 = (f32[128]{0:T(128)S(1)}, f32[8]{0:T(128)S(1)}, f32[8]{0:T(128)S(1)}, f32[128]{0:T(128)S(1)}) all-reduce(f32[128]{0:T(128)S(1)} %dynamic-update-slice.3, f32[8]{0:T(128)S(1)} %convert_dynamic-update-slice_fusion, f32[8]{0:T(128)S(1)} %convert_dynamic-update-slice_fusion.1, ...), channel_id=7, replica_groups=mesh['seq'=8,'head'=4] {'seq'}, use_global_device_ids=true, to_apply=%add.3 | all-reduce | flops 272 | bytes 2176
  172.8 5.0 %copy.149 = bf16[1536,1024]{0,1:T(8,128)(2,1)} copy(bf16[1536,1024]{1,0:T(8,128)(2,1)} %param.17) | data formatting | bytes 6291456 | tf_op args[1]
  179.2 9.2 %fusion.10 = f32[12,16,128,64]{2,3,1,0:T(8,128)} fusion(f32[16,12,128]{2,0,1:T(8,128)S(1)} %copy.123, f32[16,12,128]{2,0,1:T(8,128)S(1)} %copy.121, f32[12,128,128]{2,1,0:T(8,128)S(1)} %fusion.63, pred[12,128,128]{2,1,0:T(8,128)(4,1)S(1)} %get-tuple-element.557, bf16[12,128,16,64]{1,0,3,2:T(8,128)(2,1)} %reshape_reshape.3), kind=kOutput, calls=%fused_computation.36 | convolution fusion | flops 421527552 | bytes 10616832 | tf_op jit(solution)/shard_map/hbts,bshp->bthp/dot_general | solution.py:58
  188.4 8.6 %fusion.11 = f32[12,16,128,64]{2,3,1,0:T(8,128)} fusion(f32[16,12,128]{2,0,1:T(8,128)S(1)} %copy_bitcast_fusion.1, f32[16,12,128]{2,0,1:T(8,128)S(1)} %copy.135, f32[12,128,128]{2,1,0:T(8,128)S(1)} %fusion.64, pred[12,128,128]{2,1,0:T(8,128)(4,1)S(1)} %get-tuple-element.558, bf16[1536,16,64]{0,2,1:T(8,128)(2,1)S(1)} %copy-done.3), kind=kOutput, calls=%fused_computation.37 | convolution fusion | flops 421527552 | bytes 10616832 | tf_op jit(solution)/shard_map/hbts,bshp->bthp/dot_general | solution.py:58
  198.2 40.0 %while.69 = (s32[]{:T(128)}, f32[16,128,64]{2,1,0:T(8,128)S(1)}, f32[1]{0:T(128)}, f32[1]{0:T(128)}, s32[]{:T(128)}, /*index=5*/f32[8,16,128,64]{2,3,1,0:T(8,128...) while((s32[]{:T(128)}, f32[16,128,64]{2,1,0:T(8,128)S(1)}, ...), condition=%wide.region_9.10_spmd, body=%wide.region_8.9_spmd.sunk | while | flops 262175 | bytes 3670492 | solution.py:22
  238.3 12.6 %fusion.24 = f32[12,16,8,8,128]{4,3,2,1,0:T(8,128)} fusion(f32[12,16,128,64]{2,3,1,0:T(8,128)} %fusion.11, f32[12,128,16]{1,2,0:T(8,128)S(1)} %copy-done.9, bf16[12,128,128,1]{2,1,3,0:T(8,128)(2,1)S(1)} %bitcast.179, f32[12,16,128,64]{3,2,1,0:T(8,128)} %get-tuple-element.305, f32[16,128,64]{2,1,0:T(8,128)S(1)} %broadcast_multiply_fusion, ...), kind=kOutput, calls=%fused_computation.54 | convolution fusion | flops 410517504 | bytes 19890944 | tf_op jit(solution)/shard_map/btn,bhnp->bthp/dot_general | solution.py:104
  251.0 6.2 %copy.179 = f32[12,16,8,8,128]{4,3,0,2,1:T(8,128)} copy(f32[12,16,8,8,128]{4,3,2,1,0:T(8,128)} %fusion.24) | data formatting | bytes 12582912 | tf_op jit(solution)/shard_map/reshape | solution.py:150
  257.2 10.5 %rev.27 = f32[1536,16,64]{0,2,1:T(8,128)} reverse(f32[1536,16,64]{0,2,1:T(8,128)} %bitcast.171), dimensions={0} | reverse | bytes 12582912 | tf_op jit(solution)/shard_map/rev | solution.py:150
  268.7 13.0 %fusion.26 = f32[12,16,8,8,128]{4,3,2,1,0:T(8,128)} fusion(f32[12,16,128,64]{2,3,1,0:T(8,128)} %fusion.10, f32[12,128,16]{1,2,0:T(8,128)} %copy.133, bf16[12,128,128,1]{2,1,3,0:T(8,128)(2,1)S(1)} %bitcast.177, f32[12,16,128,64]{3,2,1,0:T(8,128)} %get-tuple-element.299, f32[16,128,64]{2,1,0:T(8,128)} %broadcast_multiply_fusion.1, f32[12,16]{1,0:T(8,128)S(1)} %copy-done.11), kind=kOutput, calls=%fused_computation.57 | convolution fusion | flops 410517504 | bytes 19890944 | tf_op jit(solution)/shard_map/btn,bhnp->bthp/dot_general | solution.py:104
  281.8 8.6 %multiply_reduce_fusion = (f32[1536]{0:T(1024)S(1)}, f32[1536,16,64]{0,2,1:T(8,128)}) fusion(f32[16]{0:T(128)S(1)} %copy-done.16, f32[1536,16,64]{0,2,1:T(8,128)} %rev.27, f32[12,16,8,8,128]{4,3,2,1,0:T(8,128)} %fusion.26, bf16[1536,1024]{0,1:T(8,128)(2,1)} %copy.149, bf16[1536,1024]{0,1:T(8,128)(2,1)S(1)} %copy-done.2), kind=kLoop, calls=%fused_computation.58 | loop fusion | flops 18872832 | bytes 25172032 | tf_op jit(solution)/shard_map/reduce_sum | solution.py:158
  290.3 12.1 %psum.7 = f32[1536]{0:T(1024)S(1)} all-reduce(f32[1536]{0:T(1024)S(1)} %get-tuple-element.537), channel_id=1, replica_groups=mesh['seq'=8,'head'=4] {'head'}, use_global_device_ids=true, to_apply=%region_11.12 | all-reduce | flops 1536 | bytes 12288 | tf_op jit(solution)/shard_map/psum | solution.py:159
  302.5 3.4 %fusion.22 = bf16[1536,1024]{0,1:T(8,128)(2,1)S(1)} fusion(f32[1536,16,64]{0,2,1:T(8,128)} %get-tuple-element.538, f32[1024]{0:T(1024)S(1)} %copy-done.15, f32[1536]{0:T(1024)S(1)} %add_rsqrt_fusion), kind=kLoop, calls=%fused_computation.51 | loop fusion | flops 4718592 | bytes 9447424 | tf_op jit(solution)/shard_map/convert_element_type | solution.py:162
  305.9 2.9 copy.150
  (242 shorter events, 105.9 us)
Async XLA Ops:
  6.5 18.9 %copy-start.8 = (s32[1536]{0:T(1024)S(1)}, s32[1536]{0:T(1024)}, u32[]{:S(2)}) copy-start(s32[1536]{0:T(1024)} %param.22) | copy-start | bytes 18436
  6.5 190.5 %all-gather.9.cloned.1.call-start = ((), (), s32[]{:S(2)}) async-start(), calls=%async_computation | async-start | bytes 4718592 | tf_op jit(solution)/shard_map/all_gather | solution.py:13
  50.6 41.0 %copy-start.5 = (bf16[1536,128]{1,0:T(8,128)(2,1)S(1)}, bf16[1536,128]{1,0:T(8,128)(2,1)}, u32[]{:S(2)}) copy-start(bf16[1536,128]{1,0:T(8,128)(2,1)} %get-tuple-element.547) | copy-start | bytes 1179652
  81.4 1.4 copy-start.12
  81.4 10.2 %copy-start.10 = (f32[12,16]{1,0:T(8,128)}, f32[12,16]{1,0:T(8,128)S(1)}, u32[]{:S(2)}) copy-start(f32[12,16]{1,0:T(8,128)S(1)} %get-tuple-element.300) | copy-start | bytes 2308
  82.6 114.6 %all-gather.11.cloned.1.call-start = ((), (), s32[]{:S(2)}) async-start(), calls=%async_computation.1 | async-start | bytes 4718592 | tf_op jit(solution)/shard_map/all_gather | solution.py:13
  112.7 6.1 %copy-start.14 = (f32[16]{0:T(128)S(1)}, f32[16]{0:T(128)}, u32[]{:S(2)}) copy-start(f32[16]{0:T(128)} %custom-call.3) | copy-start | bytes 196
  118.8 33.5 %copy-start.17 = (u32[32]{0:T(128)S(1)}, u32[32]{0:T(128)}, u32[]{:S(2)}) copy-start(u32[32]{0:T(128)} %constant.122) | copy-start | bytes 388
  118.8 34.9 %copy-start.13 = (f32[16]{0:T(128)S(1)}, f32[16]{0:T(128)}, u32[]{:S(2)}) copy-start(f32[16]{0:T(128)} %copy-done.12) | copy-start | bytes 196
  118.8 52.2 %copy-start.6 = (f32[12,128,16]{1,0,2:T(8,128)S(1)}, f32[12,128,16]{1,0,2:T(8,128)}, u32[]{:S(2)}) copy-start(f32[12,128,16]{1,0,2:T(8,128)} %get-tuple-element.553) | copy-start | bytes 294916
  118.8 53.0 %copy-start.7 = (f32[12,128,16]{1,0,2:T(8,128)S(1)}, f32[12,128,16]{1,0,2:T(8,128)}, u32[]{:S(2)}) copy-start(f32[12,128,16]{1,0,2:T(8,128)} %get-tuple-element.556) | copy-start | bytes 294916
  118.8 53.6 %copy-start.4 = (bf16[1536,128]{1,0:T(8,128)(2,1)S(1)}, bf16[1536,128]{1,0:T(8,128)(2,1)}, u32[]{:S(2)}) copy-start(bf16[1536,128]{1,0:T(8,128)(2,1)} %get-tuple-element.548) | copy-start | bytes 1179652
  179.2 9.2 %copy-start.3 = (bf16[1536,16,64]{0,2,1:T(8,128)(2,1)S(1)}, bf16[1536,16,64]{0,2,1:T(8,128)(2,1)}, u32[]{:S(2)}) copy-start(bf16[1536,16,64]{0,2,1:T(8,128)(2,1)} %rev.26) | copy-start | bytes 9437188
  197.1 0.9 copy-start
  198.2 40.1 %copy-start.9 = (f32[12,128,16]{1,2,0:T(8,128)S(1)}, f32[12,128,16]{1,2,0:T(8,128)}, u32[]{:S(2)}) copy-start(f32[12,128,16]{1,2,0:T(8,128)} %copy.147) | copy-start | bytes 294916
  257.2 10.5 %copy-start.1 = (f32[16,128,64]{2,1,0:T(8,128)S(1)}, f32[16,128,64]{2,1,0:T(8,128)}, u32[]{:S(2)}) copy-start(f32[16,128,64]{2,1,0:T(8,128)} %copy-done) | copy-start | bytes 1572868
  257.2 11.6 %copy-start.11 = (f32[12,16]{1,0:T(8,128)S(1)}, f32[12,16]{1,0:T(8,128)}, u32[]{:S(2)}) copy-start(f32[12,16]{1,0:T(8,128)} %copy-done.10) | copy-start | bytes 2308
  268.7 13.0 %copy-start.2 = (bf16[1536,1024]{0,1:T(8,128)(2,1)S(1)}, bf16[1536,1024]{0,1:T(8,128)(2,1)}, u32[]{:S(2)}) copy-start(bf16[1536,1024]{0,1:T(8,128)(2,1)} %copy.124) | copy-start | bytes 9437188
  268.7 13.0 %copy-start.16 = (f32[16]{0:T(128)S(1)}, f32[16]{0:T(128)}, u32[]{:S(2)}) copy-start(f32[16]{0:T(128)} %param.21) | copy-start | bytes 196
  281.8 20.7 %copy-start.15 = (f32[1024]{0:T(1024)S(1)}, f32[1024]{0:T(1024)}, u32[]{:S(2)}) copy-start(f32[1024]{0:T(1024)} %param.23) | copy-start | bytes 12292
Sparse Core Ops, SparseCore 0:
  82.7 39.4 all-gather.8
  151.1 39.5 all-gather.10
where the time goes:
time: 319 us; the launch traced here: 316 us
  local copies, waits for them, and re-layouts  91.5 us (29%)
  other arithmetic  91.5 us (29%)
  matrix products  65 us (20%)
  blocking collectives  27.6 us (9%)
  loops' own time  24.3 us (8%)
  between operations  15.6 us (5%)
    add x24, other arithmetic, advance(): decay_now[:, None, None] * state_now + local_now  34 us
    dynamic_update_slice x24, other arithmetic, local_pass(): lax.scan(advance, (start_state, start_factor), (local_states, block_decay))  25.9 us
    dot_general x2, matrix products, finish(): jnp.einsum('btn,bhnp->bthp', c_blocks, entering, preferred_element_type=j...  25.7 us
    another operation x2, loops' own time, prefix(): return lax.fori_loop(0, ahead, one, state)  23.8 us
    dot_general x2, matrix products, local_pass(): jnp.einsum('hbsn,bshp->bhnp', weighted_b, blocks_x, preferred_element_typ...  20.7 us
    dot_general x2, matrix products, local_pass(): jnp.einsum('hbts,bshp->bthp', weights, blocks_x, preferred_element_type=j...  17.8 us
    unnamed x1, blocking collectives  15.5 us
    dynamic_slice x21, local copies, waits for them, and re-layouts, one(): lax.dynamic_index_in_dim(a, source, 0, False)  14.6 us
  transfers between devices with their start and end apart: 2, of which 0 were waited for; matrix products, arithmetic and copies ran while one was open for 31% of the time, Pallas kernels for 0%

commit v1 on v0

--- a/solution.py
+++ b/solution.py
@@ -156,7 +156,7 @@
     gate_wide = gate_input.astype(jnp.float32).reshape(tokens, head_count, head_width)
     gated_out = (combined * jax.nn.silu(gate_wide)).reshape(tokens, head_count * head_width)
     partial_squares = jnp.sum(gated_out * gated_out, axis=1)
-    square_total = lax.psum(partial_squares, "head")
+    square_total = jnp.sum(lax.all_gather(partial_squares, "head"), axis=0)
     channels = lax.axis_size("head") * head_count * head_width
     inverse_rms = lax.rsqrt(square_total / channels + 1e-05)
     return (gated_out * inverse_rms[:, None] * norm_gain[None, :]).astype(jnp.bfloat16)

time: 319 us -> 333 us (1.044)
  other arithmetic: 91.5 us -> 108 us
    add x7, other arithmetic: 1.53 us -> 16.6 us  [combine(): state_second + carried[:, None, None] * state_first]
    all_gather x0 -> x1, blocking collectives: none -> 13.3 us  [local(): square_total = jnp.sum(lax.all_gather(partial_squares, 'head'), axis=0)]
    psum x1 -> x0, blocking collectives: 12.1 us -> none  [local(): square_total = lax.psum(partial_squares, 'head')]
    unnamed x47 -> x44, local copies, waits for them, and re-layouts: 11.8 us -> 10.9 us
  transfers between devices with their start and end apart: 2 -> 2, of which waited for: 0 -> 0; matrix products, arithmetic and copies ran while one was open for 31% -> 29% of each run, Pallas kernels for 0% -> 0%
where the time goes in v1:
time: 333 us; the launch traced here: 330 us
  other arithmetic  108 us (32%)
  local copies, waits for them, and re-layouts  90.8 us (27%)
  matrix products  65.2 us (20%)
  blocking collectives  28.8 us (9%)
  loops' own time  21.7 us (7%)
  between operations  15.6 us (5%)
    add x24, other arithmetic, advance(): decay_now[:, None, None] * state_now + local_now  34 us
    dynamic_update_slice x24, other arithmetic, local_pass(): lax.scan(advance, (start_state, start_factor), (local_states, block_decay))  25.8 us
    dot_general x2, matrix products, finish(): jnp.einsum('btn,bhnp->bthp', c_blocks, entering, preferred_element_type=j...  25.7 us
    another operation x2, loops' own time, prefix(): return lax.fori_loop(0, ahead, one, state)  21.2 us
    dot_general x2, matrix products, local_pass(): jnp.einsum('hbsn,bshp->bhnp', weighted_b, blocks_x, preferred_element_typ...  20.8 us
    dot_general x2, matrix products, local_pass(): jnp.einsum('hbts,bshp->bthp', weights, blocks_x, preferred_element_type=j...  17.9 us
    add x7, other arithmetic, combine(): state_second + carried[:, None, None] * state_first  16.6 us
    unnamed x1, blocking collectives  15.5 us
  transfers between devices with their start and end apart: 2, of which 0 were waited for; matrix products, arithmetic and copies ran while one was open for 29% of the time, Pallas kernels for 0%

profile of v1, /device:TPU:0, one launch (start us, length us, event | category | flops | bytes accessed | tf_op | source)
XLA Modules:
  0.0 329.9 jit_solution(6848693730752550988)
XLA Ops:
  15.4 4.6 %copy.124 = bf16[1536,1024]{0,1:T(8,128)(2,1)} copy(bf16[1536,1024]{1,0:T(8,128)(2,1)} %param.16) | data formatting | bytes 6291456 | tf_op args[0]
  20.0 4.5 %reduce_window_sum.17 = f32[16,12,128]{2,1,0:T(8,128)S(1)} reduce-window(f32[16,12,128]{2,1,0:T(8,128)S(1)} %reshape_squeeze.13, f32[]{:T(128)} %constant.111.clone.1), window={size=1x1x128 pad=0_0x0_0x127_0}, to_apply=%region_0.0 | reduce-window | flops 3121152 | bytes 196612 | tf_op jit(solution)/shard_map/jit(cumsum)/reduce_window_sum | solution.py:45
  26.5 6.9 %reshape_reshape.3 = bf16[12,128,16,64]{1,0,3,2:T(8,128)(2,1)} reshape(bf16[1536,1024]{0,1:T(8,128)(2,1)} %copy.124) | data formatting | bytes 6291456 | tf_op jit(solution)/shard_map/reshape;reshape | solution.py:120
  34.3 10.5 %fusion.16 = f32[12,16,128,64]{3,2,1,0:T(8,128)} fusion(f32[16,12,128]{2,0,1:T(8,128)S(1)} %copy.126, f32[12,128,128]{2,1,0:T(8,128)S(1)} %convert_element_type.77, bf16[12,128,16,64]{1,0,3,2:T(8,128)(2,1)} %reshape_reshape.3), kind=kOutput, calls=%fused_computation.42 | convolution fusion | flops 408944640 | bytes 10321920 | tf_op jit(solution)/shard_map/hbsn,bshp->bhnp/dot_general | solution.py:67
  44.8 6.1 %broadcast.147.clone.1 = f32[12,16,128,64]{3,2,1,0:T(8,128)} broadcast(f32[]{:T(128)} %constant.111.clone.1), dimensions={} | broadcast | bytes 6291460 | tf_op jit(solution)/shard_map/broadcast.7
  50.9 30.8 %while.70 = (s32[]{:T(128)}, f32[16,128,64]{2,1,0:T(8,128)S(1)}, f32[16]{0:T(128)S(1)}, f32[12,16,128,64]{3,2,1,0:T(8,128)}, f32[12,16]{1,0:T(8,128)S(1)}, /*ind...) while((s32[]{:T(128)}, f32[16,128,64]{2,1,0:T(8,128)S(1)}, ...), condition=%wide.region_2.3_spmd.clone, body=%wide.region_1.2_spmd.clone.sunk | while | flops 524323 | bytes 3146869 | solution.py:85
  84.0 4.6 %reduce_window_sum.18 = f32[16,12,128]{2,1,0:T(8,128)S(1)} reduce-window(f32[16,12,128]{2,1,0:T(8,128)S(1)} %reshape.219, f32[]{:T(128)} %constant.111.clone.1), window={size=1x1x128 pad=0_0x0_0x127_0}, to_apply=%region_5.6 | reduce-window | flops 3121152 | bytes 196612 | tf_op jit(solution)/shard_map/jit(cumsum)/reduce_window_sum | solution.py:45
  92.3 8.6 %rev.26 = bf16[1536,16,64]{0,2,1:T(8,128)(2,1)} reverse(bf16[1536,16,64]{0,2,1:T(8,128)(2,1)} %bitcast.170), dimensions={0} | reverse | bytes 6291456 | tf_op jit(solution)/shard_map/rev | solution.py:121
  102.4 10.4 %fusion.18 = f32[12,16,128,64]{3,2,1,0:T(8,128)} fusion(f32[16,12,128]{2,0,1:T(8,128)} %copy.140, f32[12,128,128]{2,1,0:T(8,128)S(1)} %convert_element_type.84, bf16[1536,16,64]{0,2,1:T(8,128)(2,1)} %rev.26), kind=kOutput, calls=%fused_computation.44 | convolution fusion | flops 408944640 | bytes 10321920 | tf_op jit(solution)/shard_map/hbsn,bshp->bhnp/dot_general | solution.py:67
  112.8 6.1 %broadcast.147.clone = f32[12,16,128,64]{3,2,1,0:T(8,128)} broadcast(f32[]{:T(128)} %constant.111.clone.1), dimensions={} | broadcast | bytes 6291460 | tf_op jit(solution)/shard_map/broadcast.7
  118.9 30.8 %while.71 = (s32[]{:T(128)}, f32[16,128,64]{2,1,0:T(8,128)S(1)}, f32[16]{0:T(128)S(1)}, f32[12,16,128,64]{3,2,1,0:T(8,128)}, f32[12,16]{1,0:T(8,128)S(1)}, /*ind...) while((s32[]{:T(128)}, f32[16,128,64]{2,1,0:T(8,128)S(1)}, ...), condition=%wide.region_7.8_spmd.clone, body=%wide.region_6.7_spmd.clone.sunk | while | flops 524323 | bytes 3146869 | solution.py:85
  155.4 15.5 %all-reduce.4 = (f32[128]{0:T(128)S(1)}, f32[8]{0:T(128)S(1)}, f32[8]{0:T(128)S(1)}, f32[128]{0:T(128)S(1)}) all-reduce(f32[128]{0:T(128)S(1)} %dynamic-update-slice.3, f32[8]{0:T(128)S(1)} %convert_dynamic-update-slice_fusion, f32[8]{0:T(128)S(1)} %convert_dynamic-update-slice_fusion.1, ...), channel_id=7, replica_groups=mesh['seq'=8,'head'=4] {'seq'}, use_global_device_ids=true, to_apply=%add.3 | all-reduce | flops 272 | bytes 2176
  172.7 4.9 %copy.149 = bf16[1536,1024]{0,1:T(8,128)(2,1)} copy(bf16[1536,1024]{1,0:T(8,128)(2,1)} %param.17) | data formatting | bytes 6291456 | tf_op args[1]
  179.1 9.2 %fusion.10 = f32[12,16,128,64]{2,3,1,0:T(8,128)} fusion(f32[16,12,128]{2,0,1:T(8,128)S(1)} %copy.123, f32[16,12,128]{2,0,1:T(8,128)S(1)} %copy.121, f32[12,128,128]{2,1,0:T(8,128)S(1)} %fusion.63, pred[12,128,128]{2,1,0:T(8,128)(4,1)S(1)} %get-tuple-element.557, bf16[12,128,16,64]{1,0,3,2:T(8,128)(2,1)} %reshape_reshape.3), kind=kOutput, calls=%fused_computation.36 | convolution fusion | flops 421527552 | bytes 10616832 | tf_op jit(solution)/shard_map/hbts,bshp->bthp/dot_general | solution.py:58
  188.3 8.7 %fusion.11 = f32[12,16,128,64]{2,3,1,0:T(8,128)} fusion(f32[16,12,128]{2,0,1:T(8,128)S(1)} %copy_bitcast_fusion.1, f32[16,12,128]{2,0,1:T(8,128)S(1)} %copy.135, f32[12,128,128]{2,1,0:T(8,128)S(1)} %fusion.64, pred[12,128,128]{2,1,0:T(8,128)(4,1)S(1)} %get-tuple-element.558, bf16[1536,16,64]{0,2,1:T(8,128)(2,1)S(1)} %copy-done.1), kind=kOutput, calls=%fused_computation.37 | convolution fusion | flops 421527552 | bytes 10616832 | tf_op jit(solution)/shard_map/hbts,bshp->bthp/dot_general | solution.py:58
  198.3 52.1 %while.69 = (s32[]{:T(128)}, f32[16,128,64]{2,1,0:T(8,128)}, f32[1]{0:T(128)}, f32[1]{0:T(128)}, s32[]{:T(128)}, /*index=5*/f32[8,16,128,64]{2,3,1,0:T(8,128)}, ...) while((s32[]{:T(128)}, f32[16,128,64]{2,1,0:T(8,128)}, ...), condition=%wide.region_9.10_spmd, body=%wide.region_8.9_spmd.sunk | while | flops 262175 | bytes 3670492 | solution.py:22
  251.7 12.6 %fusion.24 = f32[12,16,8,8,128]{4,3,2,1,0:T(8,128)} fusion(f32[12,16,128,64]{2,3,1,0:T(8,128)} %fusion.11, f32[12,128,16]{1,2,0:T(8,128)S(1)} %copy-done.7, bf16[12,128,128,1]{2,1,3,0:T(8,128)(2,1)S(1)} %bitcast.179, f32[12,16,128,64]{3,2,1,0:T(8,128)} %get-tuple-element.305, f32[16,128,64]{2,1,0:T(8,128)S(1)} %broadcast_multiply_fusion, ...), kind=kOutput, calls=%fused_computation.54 | convolution fusion | flops 410517504 | bytes 19890944 | tf_op jit(solution)/shard_map/btn,bhnp->bthp/dot_general | solution.py:104
  264.3 6.2 %copy.179 = f32[12,16,8,8,128]{4,3,0,2,1:T(8,128)} copy(f32[12,16,8,8,128]{4,3,2,1,0:T(8,128)} %fusion.24) | data formatting | bytes 12582912 | tf_op jit(solution)/shard_map/reshape | solution.py:150
  270.5 10.3 %rev.27 = f32[1536,16,64]{0,2,1:T(8,128)} reverse(f32[1536,16,64]{0,2,1:T(8,128)} %bitcast.171), dimensions={0} | reverse | bytes 12582912 | tf_op jit(solution)/shard_map/rev | solution.py:150
  281.9 13.0 %fusion.26 = f32[12,16,8,8,128]{4,3,2,1,0:T(8,128)} fusion(f32[12,16,128,64]{2,3,1,0:T(8,128)} %fusion.10, f32[12,128,16]{1,2,0:T(8,128)} %copy.133, bf16[12,128,128,1]{2,1,3,0:T(8,128)(2,1)S(1)} %bitcast.177, f32[12,16,128,64]{3,2,1,0:T(8,128)} %get-tuple-element.299, f32[16,128,64]{2,1,0:T(8,128)} %broadcast_multiply_fusion.1, f32[12,16]{1,0:T(8,128)S(1)} %copy-done.9), kind=kOutput, calls=%fused_computation.57 | convolution fusion | flops 410517504 | bytes 19890944 | tf_op jit(solution)/shard_map/btn,bhnp->bthp/dot_general | solution.py:104
  294.9 8.5 %multiply_reduce_fusion = (f32[1536]{0:T(1024)S(1)}, f32[1536,16,64]{0,2,1:T(8,128)}) fusion(f32[16]{0:T(128)S(1)} %copy-done.14, f32[1536,16,64]{0,2,1:T(8,128)} %rev.27, f32[12,16,8,8,128]{4,3,2,1,0:T(8,128)} %fusion.26, bf16[1536,1024]{0,1:T(8,128)(2,1)} %copy.149, bf16[1536,1024]{0,1:T(8,128)(2,1)S(1)} %copy-done), kind=kLoop, calls=%fused_computation.58 | loop fusion | flops 18872832 | bytes 25172032 | tf_op jit(solution)/shard_map/reduce_sum | solution.py:158
  303.5 13.3 %all-gather.7 = f32[4,1,1536]{2,1,0:T(1,128)S(1)} all-gather(f32[1,1,1536]{2,1,0:T(1,128)S(1)} %reshape.253), channel_id=8, replica_groups=mesh['seq'=8,'head'=4] {'head'}, dimensions={0}, use_global_device_ids=true | all-gather | bytes 30720 | tf_op jit(solution)/shard_map/all_gather | solution.py:159
  316.8 3.4 %fusion.22 = bf16[1536,1024]{0,1:T(8,128)(2,1)S(1)} fusion(f32[1536,16,64]{0,2,1:T(8,128)} %get-tuple-element.538, f32[1024]{0:T(1024)S(1)} %copy-done.13, f32[1536]{0:T(1024)S(1)} %add_rsqrt_fusion), kind=kLoop, calls=%fused_computation.51 | loop fusion | flops 4718592 | bytes 9447424 | tf_op jit(solution)/shard_map/convert_element_type | solution.py:162
  320.2 2.9 copy.150
  (240 shorter events, 121.8 us)
Async XLA Ops:
  6.5 19.1 %copy-start.6 = (s32[1536]{0:T(1024)S(1)}, s32[1536]{0:T(1024)}, u32[]{:S(2)}) copy-start(s32[1536]{0:T(1024)} %param.22) | copy-start | bytes 18436
  6.5 190.5 %all-gather.11.cloned.1.call-start = ((), (), s32[]{:S(2)}) async-start(), calls=%async_computation | async-start | bytes 4718592 | tf_op jit(solution)/shard_map/all_gather | solution.py:13
  50.9 40.9 %copy-start.3 = (bf16[1536,128]{1,0:T(8,128)(2,1)S(1)}, bf16[1536,128]{1,0:T(8,128)(2,1)}, u32[]{:S(2)}) copy-start(bf16[1536,128]{1,0:T(8,128)(2,1)} %get-tuple-element.547) | copy-start | bytes 1179652
  81.7 1.4 copy-start.10
  81.7 10.1 %copy-start.8 = (f32[12,16]{1,0:T(8,128)}, f32[12,16]{1,0:T(8,128)S(1)}, u32[]{:S(2)}) copy-start(f32[12,16]{1,0:T(8,128)S(1)} %get-tuple-element.300) | copy-start | bytes 2308
  82.9 114.3 %all-gather.13.cloned.1.call-start = ((), (), s32[]{:S(2)}) async-start(), calls=%async_computation.1 | async-start | bytes 4718592 | tf_op jit(solution)/shard_map/all_gather | solution.py:13
  112.8 6.1 %copy-start.12 = (f32[16]{0:T(128)S(1)}, f32[16]{0:T(128)}, u32[]{:S(2)}) copy-start(f32[16]{0:T(128)} %custom-call.3) | copy-start | bytes 196
  118.9 33.4 %copy-start.15 = (u32[32]{0:T(128)S(1)}, u32[32]{0:T(128)}, u32[]{:S(2)}) copy-start(u32[32]{0:T(128)} %constant.122) | copy-start | bytes 388
  118.9 34.9 %copy-start.11 = (f32[16]{0:T(128)S(1)}, f32[16]{0:T(128)}, u32[]{:S(2)}) copy-start(f32[16]{0:T(128)} %copy-done.10) | copy-start | bytes 196
  118.9 52.1 %copy-start.4 = (f32[12,128,16]{1,0,2:T(8,128)S(1)}, f32[12,128,16]{1,0,2:T(8,128)}, u32[]{:S(2)}) copy-start(f32[12,128,16]{1,0,2:T(8,128)} %get-tuple-element.553) | copy-start | bytes 294916
  118.9 52.8 %copy-start.5 = (f32[12,128,16]{1,0,2:T(8,128)S(1)}, f32[12,128,16]{1,0,2:T(8,128)}, u32[]{:S(2)}) copy-start(f32[12,128,16]{1,0,2:T(8,128)} %get-tuple-element.556) | copy-start | bytes 294916
  118.9 53.5 %copy-start.2 = (bf16[1536,128]{1,0:T(8,128)(2,1)S(1)}, bf16[1536,128]{1,0:T(8,128)(2,1)}, u32[]{:S(2)}) copy-start(bf16[1536,128]{1,0:T(8,128)(2,1)} %get-tuple-element.548) | copy-start | bytes 1179652
  179.1 9.2 %copy-start.1 = (bf16[1536,16,64]{0,2,1:T(8,128)(2,1)S(1)}, bf16[1536,16,64]{0,2,1:T(8,128)(2,1)}, u32[]{:S(2)}) copy-start(bf16[1536,16,64]{0,2,1:T(8,128)(2,1)} %rev.26) | copy-start | bytes 9437188
  198.3 53.4 %copy-start.7 = (f32[12,128,16]{1,2,0:T(8,128)S(1)}, f32[12,128,16]{1,2,0:T(8,128)}, u32[]{:S(2)}) copy-start(f32[12,128,16]{1,2,0:T(8,128)} %copy.147) | copy-start | bytes 294916
  270.5 11.4 %copy-start.9 = (f32[12,16]{1,0:T(8,128)S(1)}, f32[12,16]{1,0:T(8,128)}, u32[]{:S(2)}) copy-start(f32[12,16]{1,0:T(8,128)} %copy-done.8) | copy-start | bytes 2308
  281.9 13.0 %copy-start = (bf16[1536,1024]{0,1:T(8,128)(2,1)S(1)}, bf16[1536,1024]{0,1:T(8,128)(2,1)}, u32[]{:S(2)}) copy-start(bf16[1536,1024]{0,1:T(8,128)(2,1)} %copy.124) | copy-start | bytes 9437188
  281.9 13.0 %copy-start.14 = (f32[16]{0:T(128)S(1)}, f32[16]{0:T(128)}, u32[]{:S(2)}) copy-start(f32[16]{0:T(128)} %param.21) | copy-start | bytes 196
  294.9 21.9 %copy-start.13 = (f32[1024]{0:T(1024)S(1)}, f32[1024]{0:T(1024)}, u32[]{:S(2)}) copy-start(f32[1024]{0:T(1024)} %param.23) | copy-start | bytes 12292
Sparse Core Ops, SparseCore 0:
  83.0 39.4 all-gather.10
  151.0 39.5 all-gather.12
